TPU v7x, 32 devices: a whole 2x2x4 slice. The times are simulated.
32 devices in a mesh: section: 2 (over x), ep: 8 (over z, y), tp: 2 (over core).
Axes of the slice: x: 2, y: 2, z: 4, core: 2. Of those that a mesh axis runs over, the one named last changes fastest.
Arguments:
- section_rows: bfloat16 [2, 32, 7168], P('section', 'ep', 'tp'), may hold values from -6 to 6
- routes: int32 [2, 32, 2], P('section', 'ep'), may hold values from 0 to 3, all different within a row; in each aligned block of 4 rows (0 to 3, 4 to 7, ..., all dimensions but the last counted through in order) at most 3 rows name the same one
- route_weights: float32 [2, 32, 2], P('section', 'ep'), may hold values from 0.1 to 0.5
- in_gain: bfloat16 [2, 7168], P('section', 'tp'), may hold values from 0.099609375 to 1.8984375
- gate_up: bfloat16 [2, 8, 7168, 2048], P('section', 'ep', 'tp'), may hold values from -0.0625 to 0.0625
- down: bfloat16 [2, 8, 1024, 7168], P('section', 'ep', None, 'tp'), may hold values from -0.125 to 0.125
- out_gain: bfloat16 [2, 7168], P('section', 'tp'), may hold values from 0.099609375 to 1.8984375
Outputs:
- layer_out: bfloat16 [2, 32, 7168], P('section', 'ep', 'tp')
- handed: bfloat16 [2, 32, 7168], P('section', 'ep', 'tp')
Inputs may be any that keep to these rules, and one draw needn't show every extreme that they name: `routes`: each row names 2 different experts. Among the 4 rows of one index of ep (aligned blocks of rows, both groups counted in order), no expert is named by more than 3 rows, a bound that some block reaches.
All inputs are finite; a program needn't handle non-finite values.
Results may differ from a plain program's by a relative error of at most 0.012.
Values may be sent and summed in bfloat16 or wider, within the bound.
A program may use at most 64 MiB of HBM per device.

v0:
```python
import jax
import jax.numpy as jnp
from jax import lax
from jax.sharding import PartitionSpec as P


def swapped(block, axis, bit):
    count = lax.axis_size(axis)
    route = []
    for low in range(count):
        high = low | 1 << bit
        if high != low and high < count:
            route += [(low, high), (high, low)]
    return lax.ppermute(block, axis, route)


def rms_scale(values):
    totals = lax.psum(jnp.sum(values * values, axis=1), "tp")
    return lax.rsqrt(totals / (values.shape[1] * lax.axis_size("tp")) + 1e-06)


def expert_block(received, gate_block, down_block):
    hidden_units = down_block.shape[0]
    partial_sums = jnp.einsum(
        "smd,dh->smh", received, gate_block, preferred_element_type=jnp.float32
    )
    totals = lax.psum(partial_sums, "tp")
    hidden = (jax.nn.silu(totals[..., :hidden_units]) * totals[..., hidden_units:]).astype(
        jnp.bfloat16
    )
    return jnp.einsum("smh,hd->smd", hidden, down_block, preferred_element_type=jnp.float32).astype(
        jnp.bfloat16
    )


def body(section_rows, routes, route_weights, in_gain, gate_up, down, out_gain):
    inputs = section_rows[0]
    row_count, half_width = inputs.shape
    topk = routes.shape[2]
    ep_size = lax.axis_size("ep")
    share_count = min(16, ep_size // 4)
    expert_count = ep_size // share_count
    capacity = min(row_count, 3 * row_count * topk // (2 * expert_count))
    values = inputs.astype(jnp.float32)
    normed = (values * rms_scale(values)[:, None] * in_gain[0].astype(jnp.float32)[None, :]).astype(
        jnp.bfloat16
    )
    flat_ids = routes[0].reshape(-1)
    onehot = (flat_ids[:, None] == jnp.arange(expert_count, dtype=jnp.int32)[None, :]).astype(
        jnp.int32
    )
    slot_rank = jnp.sum((jnp.cumsum(onehot, axis=0) - 1) * onehot, axis=1)
    slot_ids = flat_ids * capacity + slot_rank
    source_rows = jnp.full((expert_count * capacity,), row_count, jnp.int32)
    source_rows = source_rows.at[slot_ids].set(
        jnp.arange(row_count * topk, dtype=jnp.int32) // topk
    )
    padded = jnp.concatenate([normed, jnp.zeros((1, half_width), jnp.bfloat16)], axis=0)
    per_expert = padded[source_rows].reshape(expert_count, capacity, half_width)
    outgoing = jnp.repeat(per_expert, share_count, axis=0)
    gate_block = gate_up[0, 0]
    down_block = down[0, 0]
    received = lax.all_to_all(outgoing, "ep", split_axis=0, concat_axis=0, tiled=True)
    returned = lax.all_to_all(
        expert_block(received, gate_block, down_block),
        "ep",
        split_axis=0,
        concat_axis=0,
        tiled=True,
    )
    grouped = returned.reshape(expert_count, share_count, capacity, half_width)
    summed = jnp.sum(grouped.astype(jnp.float32), axis=1).reshape(
        expert_count * capacity, half_width
    )
    picked = summed[slot_ids]
    weighted = picked * route_weights[0].reshape(-1)[:, None]
    mixture = jnp.sum(weighted.reshape(row_count, topk, half_width), axis=1)
    layer_out = (values + mixture).astype(jnp.bfloat16)
    residual = layer_out.astype(jnp.float32)
    closing = (
        residual * rms_scale(residual)[:, None] * out_gain[0].astype(jnp.float32)[None, :]
    ).astype(jnp.bfloat16)
    handed = swapped(closing, "section", 0)
    return (layer_out[None], handed[None])


def solution(mesh):
    return jax.shard_map(
        body,
        mesh=mesh,
        in_specs=(
            P("section", "ep", "tp"),
            P("section", "ep", None),
            P("section", "ep", None),
            P("section", "tp"),
            P("section", "ep", "tp", None),
            P("section", "ep", None, "tp"),
            P("section", "tp"),
        ),
        out_specs=(P("section", "ep", "tp"), P("section", "ep", "tp")),
        check_vma=False,
    )
```

profile of v0, /device:TPU:0, one launch (start us, length us, event | category | flops | bytes accessed | tf_op | source)
XLA Modules:
  0.0 91.3 jit_solution(17942920995727505197)
XLA Ops:
  7.2 0.8 copy.25
  8.0 0.7 broadcast_multiply_fusion
  8.7 0.1 eq.15
  8.8 0.2 reduce_window_sum.11
  9.0 0.1 copy.24
  9.1 0.1 mul.90
  9.2 0.6 scatter_custom_fusion
  9.8 0.8 convert_reduce_fusion.2
  10.5 0.9 fusion.12
  11.4 2.6 %psum.21 = f32[4]{0:T(128)S(1)} all-reduce(f32[4]{0:T(128)S(1)} %fusion.12), channel_id=1, replica_groups=mesh['section'=2,'ep'=8,'tp'=2] {'tp'}, use_global_device_ids=true, to_apply=%region_1.0 | all-reduce | flops 4 | bytes 32 | tf_op jit(solution)/shard_map/psum | solution.py:18
  14.0 0.8 fusion.14
  14.9 0.6 gather_fusion
  15.7 15.7 %all_to_all.10 = bf16[8,3,3584]{2,1,0:T(4,128)(2,1)S(1)} all-to-all(bf16[8,3,3584]{2,1,0:T(4,128)(2,1)S(1)} %bitcast.46), channel_id=1, replica_groups=mesh['section'=2,'ep'=8,'tp'=2] {'ep'}, dimensions={0} | all-to-all | bytes 344064 | tf_op jit(solution)/shard_map/all_to_all | solution.py:63
  31.4 7.9 %fusion = f32[8,3,2048]{2,0,1:T(8,128)} fusion(bf16[1,1,3584,2048]{3,2,1,0:T(8,128)(2,1)} %param.11, bf16[8,3,3584]{2,1,0:T(4,128)(2,1)S(1)} %all_to_all.10), kind=kOutput, calls=%fused_computation.3 | convolution fusion | flops 352321536 | bytes 15048704 | tf_op jit(solution)/shard_map/smd,dh->smh/dot_general | solution.py:24
  39.3 17.0 %all-reduce.3.cloned.1.call-done = f32[8,3,2048]{2,0,1:T(8,128)} async-done(((f32[8,3,2048]{2,0,1:T(8,128)}), f32[8,3,2048]{2,0,1:T(8,128)}) %all-reduce.3.cloned.1.call-update) | async-done | bytes 196624 | tf_op jit(solution)/shard_map/psum | solution.py:27
  56.3 4.3 %fusion.4 = bf16[8,3,3584]{2,0,1:T(8,128)(2,1)S(1)} fusion(bf16[1,1,1024,3584]{3,2,1,0:T(8,128)(2,1)} %param.12, f32[8,3,2048]{2,0,1:T(8,128)} %all-reduce.3.cloned.1.call-done), kind=kOutput, calls=%fused_computation.7 | convolution fusion | flops 176394240 | bytes 7708672 | tf_op jit(solution)/shard_map/smh,hd->smd/dot_general | solution.py:31
  60.5 0.8 copy.27
  61.3 5.8 %all-to-all-start.1 = ((bf16[8,3,3584]{2,1,0:T(4,128)(2,1)}), bf16[8,3,3584]{2,1,0:T(4,128)(2,1)S(1)}, u32[]{:S(2)}, u32[]{:S(2)}) async-start(bf16[8,3,3584]{2,1,0:T(4,128)(2,1)} %copy.27), calls=%async_computation.1 | async-start | bytes 458752 | tf_op jit(solution)/shard_map/all_to_all | solution.py:64
  67.1 0.1 copy.30
  67.2 8.8 %all-to-all-done.1 = bf16[8,3,3584]{2,1,0:T(4,128)(2,1)S(1)} async-done(((bf16[8,3,3584]{2,1,0:T(4,128)(2,1)}), bf16[8,3,3584]{2,1,0:T(4,128)(2,1)S(1)}, u32[]{:S(2)}, u32[]{:S(2)}) %all-to-all-start.1) | async-done | bytes 172064 | tf_op jit(solution)/shard_map/all_to_all | solution.py:64
  76.0 0.1 convert_reduce_fusion
  76.1 0.1 reshape.60
  76.2 0.6 gather_fusion.1
  76.8 0.1 gather.10
  76.9 0.2 multiply_reduce_fusion
  77.1 0.1 fusion.17
  77.3 2.5 %psum.23 = f32[4]{0:T(128)S(1)} all-reduce(f32[4]{0:T(128)S(1)} %fusion.17), channel_id=1, replica_groups=mesh['section'=2,'ep'=8,'tp'=2] {'tp'}, use_global_device_ids=true, to_apply=%region_9.10 | all-reduce | flops 4 | bytes 32 | tf_op jit(solution)/shard_map/psum | solution.py:18
  79.8 0.1 fusion.19
  79.9 1.5 %collective-permute-start = (bf16[4,3584]{1,0:T(4,128)(2,1)S(1)}, bf16[4,3584]{1,0:T(4,128)(2,1)S(1)}, u32[]{:S(2)}, u32[]{:S(2)}) collective-permute-start(bf16[4,3584]{1,0:T(4,128)(2,1)S(1)} %fusion.19), channel_id=1, source_target_pairs={{0,16},{16,0},{1,17},{17,1},{2,18},{18,2},{3,19},{19,3},{4,20},{20... | collective-permute-start | bytes 86024 | tf_op jit(solution)/shard_map/ppermute | solution.py:14
  81.5 0.6 fusion.16
  82.1 1.8 %collective-permute-done = bf16[4,3584]{1,0:T(4,128)(2,1)S(1)} collective-permute-done((bf16[4,3584]{1,0:T(4,128)(2,1)S(1)}, bf16[4,3584]{1,0:T(4,128)(2,1)S(1)}, u32[]{:S(2)}, u32[]{:S(2)}) %collective-permute-start) | collective-permute-done | bytes 28704 | tf_op jit(solution)/shard_map/ppermute | solution.py:14
  83.9 0.6 copy.36
  (21 shorter events, 0.3 us)
Async XLA Ops:
  7.2 60.0 %copy-start.2 = (f32[1,4,2]{1,2,0:T(2,128)S(1)}, f32[1,4,2]{1,2,0:T(2,128)}, u32[]{:S(2)}) copy-start(f32[1,4,2]{1,2,0:T(2,128)} %param.9) | copy-start | bytes 100
  7.2 49.1 %all-reduce.3.cloned.1.call-start = ((), (), s32[]{:S(2)}) async-start(), calls=%async_computation.2 | async-start | bytes 393216 | tf_op jit(solution)/shard_map/psum | solution.py:27
  15.6 61.5 %copy-start = (bf16[1,4,3584]{2,1,0:T(4,128)(2,1)S(1)}, bf16[1,4,3584]{2,1,0:T(4,128)(2,1)}, u32[]{:S(2)}) copy-start(bf16[1,4,3584]{2,1,0:T(4,128)(2,1)} %param.7) | copy-start | bytes 86020
  15.6 61.6 %copy-start.1 = (bf16[1,3584]{1,0:T(2,128)(2,1)S(1)}, bf16[1,3584]{1,0:T(2,128)(2,1)}, u32[]{:S(2)}) copy-start(bf16[1,3584]{1,0:T(2,128)(2,1)} %param.13) | copy-start | bytes 21508
  61.3 14.7 %all-to-all-start.1 = ((bf16[8,3,3584]{2,1,0:T(4,128)(2,1)}), bf16[8,3,3584]{2,1,0:T(4,128)(2,1)S(1)}, u32[]{:S(2)}, u32[]{:S(2)}) async-start(bf16[8,3,3584]{2,1,0:T(4,128)(2,1)} %copy.27), calls=%async_computation.1 | async-start | bytes 458752 | tf_op jit(solution)/shard_map/all_to_all | solution.py:64
  79.9 3.9 %collective-permute-start = (bf16[4,3584]{1,0:T(4,128)(2,1)S(1)}, bf16[4,3584]{1,0:T(4,128)(2,1)S(1)}, u32[]{:S(2)}, u32[]{:S(2)}) collective-permute-start(bf16[4,3584]{1,0:T(4,128)(2,1)S(1)} %fusion.19), channel_id=1, source_target_pairs={{0,16},{16,0},{1,17},{17,1},{2,18},{18,2},{3,19},{19,3},{4,20},{20... | collective-permute-start | bytes 86024 | tf_op jit(solution)/shard_map/ppermute | solution.py:14
Sparse Core Ops, SparseCore 0:
  39.4 16.8 all-reduce.2
where the time goes:
time: 91.9 us; the launch traced here: 91.3 us
  waiting for transfers between devices  27.6 us (30%)
  blocking collectives  20.8 us (23%)
  between operations  14.2 us (15%)
  matrix products  12.1 us (13%)
  starting transfers between devices  7.34 us (8%)
  other arithmetic  4.66 us (5%)
  local copies, waits for them, and re-layouts  4.65 us (5%)
    psum x1, waiting for transfers between devices, expert_block(): totals = lax.psum(partial_sums, 'tp')  17 us
    all_to_all x1, blocking collectives, body(): lax.all_to_all(outgoing, 'ep', split_axis=0, concat_axis=0, tiled=True)  15.7 us
    all_to_all x1, waiting for transfers between devices, body(): lax.all_to_all(expert_block(received, gate_block, down_block), 'ep', spli...  8.8 us
    dot_general x1, matrix products, expert_block(): jnp.einsum('smd,dh->smh', received, gate_block, preferred_element_type=jn...  7.86 us
    all_to_all x1, starting transfers between devices, body(): lax.all_to_all(expert_block(received, gate_block, down_block), 'ep', spli...  5.77 us
    psum x2, blocking collectives, rms_scale(): totals = lax.psum(jnp.sum(values * values, axis=1), 'tp')  5.06 us
    dot_general x1, matrix products, expert_block(): jnp.einsum('smh,hd->smd', hidden, down_block, preferred_element_type=jnp....  4.25 us
  transfers between devices with their start and end apart: 3, of which 3 were waited for; matrix products, arithmetic and copies ran while one was open for 1% of the time, Pallas kernels for 0%

commit v1 on v0

v1 whole, which is shorter than its diff:
```python
import jax
import jax.numpy as jnp
from jax import lax
from jax.experimental import pallas as pl
from jax.experimental.pallas import tpu as pltpu
from jax.sharding import PartitionSpec as P

MESH = pl.DeviceIdType.MESH
EPS = 1e-06


def looped(count, step, carry=0):
    if count <= 8:
        for at in range(count):
            carry = step(at, carry)
        return carry
    return lax.fori_loop(0, count, step, carry)


def remote(src, dst, send, recv, target):
    return pltpu.make_async_remote_copy(
        src_ref=src,
        dst_ref=dst,
        send_sem=send,
        recv_sem=recv,
        device_id=target,
        device_id_type=MESH,
    )


def kernel(
    share_count,
    x_ref,
    routes_ref,
    rw_ref,
    in_gain_ref,
    out_gain_ref,
    gate_hbm,
    down_hbm,
    lo_ref,
    handed_ref,
    gate_v,
    down_v,
    rows_v,
    lhs_v,
    sq_own,
    sq_far,
    sums_own,
    sums_far,
    hidden_v,
    y_v,
    part_v,
    ret_v,
    gain_own,
    gain_far,
    lo_far,
    tot_own,
    tot_tp,
    tot_far,
    tot_diag,
    gate_sem,
    down_sem,
    rows_send,
    rows_recv,
    ret_send,
    ret_recv,
    sums_send,
    sums_recv,
    small_send,
    small_recv,
):
    n = rows_v.shape[0]
    rows, width = y_v.shape
    near = x_ref.shape[0]
    hidden = down_v.shape[0]
    span = gate_v.shape[1]
    pieces = sums_own.shape[0]
    cut = sums_own.shape[2]
    model = 2 * width
    section = lax.axis_index("section")
    me = lax.axis_index("ep")
    core = lax.axis_index("tp")
    twin = {"tp": 1 - core}
    across = {"section": 1 - section}
    diagonal = {"section": 1 - section, "tp": 1 - core}

    half = pieces // 2

    def columns(at):
        start = (at // 2) * cut + (at % 2) * hidden
        return slice(start, start + cut)

    gate_copies = [
        pltpu.make_async_copy(
            gate_hbm.at[:, columns(at)], gate_v.at[:, columns(at)], gate_sem.at[at]
        )
        for at in range(pieces)
    ]
    down_copies = [
        pltpu.make_async_copy(
            down_hbm.at[at * cut : (at + 1) * cut], down_v.at[at * cut : (at + 1) * cut], down_sem.at[at]
        )
        for at in range(half)
    ]
    for copy in gate_copies + down_copies:
        copy.start()

    barrier = pltpu.get_barrier_semaphore()

    def greet(step, carry):
        pl.semaphore_signal(
            barrier, inc=1, device_id={"ep": (me + 1 + step) % n}, device_id_type=MESH
        )
        return carry

    looped(n - 1, greet)
    for target in (twin, across, diagonal):
        pl.semaphore_signal(barrier, inc=1, device_id=target, device_id_type=MESH)
    gain_own[...] = out_gain_ref[...].astype(jnp.float32)
    rows_v[me] = x_ref[...]
    pl.semaphore_wait(barrier, n + 2)

    def rows_copy(peer):
        return remote(
            x_ref, rows_v.at[me], rows_send.at[peer], rows_recv.at[me], {"ep": peer}
        )

    def rows_arrival(peer):
        return remote(
            x_ref, rows_v.at[peer], rows_send.at[peer], rows_recv.at[peer], {"ep": peer}
        )

    def send_rows(step, carry):
        rows_copy((me + 1 + step) % n).start()
        return carry

    looped(n - 1, send_rows)
    gain_copy = remote(gain_own, gain_far, small_send.at[0], small_recv.at[0], across)
    gain_copy.start()

    def wait_rows(step, carry):
        rows_arrival((me + 1 + step) % n).wait_recv()
        return carry

    looped(n - 1, wait_rows)

    gain = in_gain_ref[...].astype(jnp.float32)
    group = 16 // near

    def build(at, carry):
        block = jnp.concatenate(
            [rows_v[at * group + i].astype(jnp.float32) for i in range(group)], axis=0
        )
        where = pl.ds(at * 16 if isinstance(at, int) else pl.multiple_of(at * 16, 16), 16)
        squares = jnp.sum(block * block, axis=1, keepdims=True)
        sq_own[where, :] = jnp.broadcast_to(squares, (16, 128))
        lhs_v[where, :] = (block * gain).astype(jnp.bfloat16)
        return carry

    looped(n // group, build)
    sq_copy = remote(sq_own, sq_far, small_send.at[1], small_recv.at[1], twin)
    sq_copy.start()

    sums_copies = []
    for at in range(pieces):
        gate_copies[at].wait()
        sums_own[at] = jnp.dot(
            lhs_v[...], gate_v[:, columns(at)], preferred_element_type=jnp.float32
        )
        copy = remote(
            sums_own.at[at], sums_far.at[at], sums_send.at[at], sums_recv.at[at], twin
        )
        copy.start()
        sums_copies.append(copy)

    sq_copy.wait_recv()
    scale = lax.rsqrt((sq_own[:, :1] + sq_far[:, :1]) / model + EPS)
    for at in range(half):
        sums_copies[2 * at].wait_recv()
        sums_copies[2 * at + 1].wait_recv()
        a = (sums_own[2 * at] + sums_far[2 * at]) * scale
        b = (sums_own[2 * at + 1] + sums_far[2 * at + 1]) * scale
        hidden_v[:, at * cut : (at + 1) * cut] = (a / (1.0 + jnp.exp(-a)) * b).astype(
            jnp.bfloat16
        )
    for copy in down_copies:
        copy.wait()

    tile = 512 if width % 512 == 0 else 128
    tiles = width // tile
    bounds = [0, (tiles + 1) // 2 * tile, width]

    def ret_copy(peer, part):
        where = slice(bounds[part], bounds[part + 1])
        return remote(
            part_v.at[peer, :, where],
            ret_v.at[me, :, where],
            ret_send.at[part, peer],
            ret_recv.at[part, me],
            {"ep": peer},
        )

    def ret_arrival(peer, part):
        where = slice(bounds[part], bounds[part + 1])
        return remote(
            part_v.at[peer, :, where],
            ret_v.at[peer, :, where],
            ret_send.at[part, peer],
            ret_recv.at[part, peer],
            {"ep": peer},
        )

    pair = 8 // near
    for part in range(2):
        low, high = bounds[part], bounds[part + 1]
        for start in range(low, high, tile):
            y_v[:, start : start + tile] = jnp.dot(
                hidden_v[...], down_v[:, start : start + tile], preferred_element_type=jnp.float32
            )

        def split(at, carry):
            where = pl.ds(at * 8 if isinstance(at, int) else pl.multiple_of(at * 8, 8), 8)
            block = y_v[where, low:high]
            for i in range(pair):
                part_v[at * pair + i, :, low:high] = block[i * near : (i + 1) * near].astype(
                    jnp.bfloat16
                )
            return carry

        looped(n // pair, split)

        def send_ret(step, carry):
            ret_copy((me + 1 + step) % n, part).start()
            return carry

        looped(n - 1, send_ret)
        ret_v[me, :, low:high] = part_v[me, :, low:high]

    named = routes_ref[...]
    weights = rw_ref[...]
    squares = jnp.zeros((near, 1), jnp.float32)
    for part in range(2):
        low, high = bounds[part], bounds[part + 1]

        def wait_ret(step, carry):
            ret_arrival((me + 1 + step) % n, part).wait_recv()
            return carry

        looped(n - 1, wait_ret)

        def add(at, total):
            weight = jnp.sum(
                jnp.where(named == at // share_count, weights, 0.0), axis=1, keepdims=True
            )
            return total + weight * ret_v[at, :, low:high].astype(jnp.float32)

        mixture = looped(n, add, jnp.zeros((near, high - low), jnp.float32))
        out = (x_ref[:, low:high].astype(jnp.float32) + mixture).astype(jnp.bfloat16)
        lo_ref[:, low:high] = out
        residual = out.astype(jnp.float32)
        squares = squares + jnp.sum(residual * residual, axis=1, keepdims=True)
    tot_own[...] = jnp.broadcast_to(squares, tot_own.shape)
    tail = [
        remote(lo_ref, lo_far, small_send.at[2], small_recv.at[2], across),
        remote(tot_own, tot_far, small_send.at[3], small_recv.at[3], across),
        remote(tot_own, tot_diag, small_send.at[4], small_recv.at[4], diagonal),
    ]
    for copy in tail:
        copy.start()
    gain_copy.wait_recv()
    for copy in tail:
        copy.wait_recv()
    final = lax.rsqrt((tot_far[:, :1] + tot_diag[:, :1]) / model + EPS)
    handed_ref[...] = (lo_far[...].astype(jnp.float32) * final * gain_far[...]).astype(
        jnp.bfloat16
    )

    for copy in [gain_copy, sq_copy] + sums_copies + tail:
        copy.wait_send()

    def drain(step, carry):
        peer = (me + 1 + step) % n
        rows_copy(peer).wait_send()
        for part in range(2):
            ret_copy(peer, part).wait_send()
        return carry

    looped(n - 1, drain)


def body(section_rows, routes, route_weights, in_gain, gate_up, down, out_gain):
    near, width = section_rows.shape[1:]
    hidden = down.shape[2]
    span = gate_up.shape[3]
    n = lax.axis_size("ep")
    share_count = min(16, n // 4)
    rows = n * near
    cut = min(512, hidden)
    pieces = span // cut
    vmem = pl.BlockSpec(memory_space=pltpu.VMEM)
    hbm = pl.BlockSpec(memory_space=pl.ANY)
    f32, bf16 = jnp.float32, jnp.bfloat16
    dma = pltpu.SemaphoreType.DMA
    layer_out, handed = pl.pallas_call(
        lambda *refs: kernel(share_count, *refs),
        out_shape=[jax.ShapeDtypeStruct((near, width), bf16)] * 2,
        in_specs=[vmem] * 5 + [hbm] * 2,
        out_specs=[vmem] * 2,
        scratch_shapes=[
            pltpu.VMEM((width, span), bf16),
            pltpu.VMEM((hidden, width), bf16),
            pltpu.VMEM((n, near, width), bf16),
            pltpu.VMEM((rows, width), bf16),
            pltpu.VMEM((rows, 128), f32),
            pltpu.VMEM((rows, 128), f32),
            pltpu.VMEM((pieces, rows, cut), f32),
            pltpu.VMEM((pieces, rows, cut), f32),
            pltpu.VMEM((rows, hidden), bf16),
            pltpu.VMEM((rows, width), f32),
            pltpu.VMEM((n, near, width), bf16),
            pltpu.VMEM((n, near, width), bf16),
            pltpu.VMEM((1, width), f32),
            pltpu.VMEM((1, width), f32),
            pltpu.VMEM((near, width), bf16),
            pltpu.VMEM((near, 128), f32),
            pltpu.VMEM((near, 128), f32),
            pltpu.VMEM((near, 128), f32),
            pltpu.VMEM((near, 128), f32),
            dma((pieces,)),
            dma((pieces // 2,)),
            dma((n,)),
            dma((n,)),
            dma((2, n)),
            dma((2, n)),
            dma((pieces,)),
            dma((pieces,)),
            dma((5,)),
            dma((5,)),
        ],
        compiler_params=pltpu.CompilerParams(
            collective_id=0, has_side_effects=True, vmem_limit_bytes=56 * 2**20
        ),
        name="routed_layer",
    )(section_rows[0], routes[0], route_weights[0], in_gain, out_gain, gate_up[0, 0], down[0, 0])
    return (layer_out[None], handed[None])


def solution(mesh):
    return jax.shard_map(
        body,
        mesh=mesh,
        in_specs=(
            P("section", "ep", "tp"),
            P("section", "ep", None),
            P("section", "ep", None),
            P("section", "tp"),
            P("section", "ep", "tp", None),
            P("section", "ep", None, "tp"),
            P("section", "tp"),
        ),
        out_specs=(P("section", "ep", "tp"), P("section", "ep", "tp")),
        check_vma=False,
    )
```

time: 91.9 us -> 35.1 us (0.38)
  Pallas kernels: 0 us -> 28.7 us
  waiting for transfers between devices: 27.6 us -> 0 us
  blocking collectives: 20.8 us -> 0 us
  between operations: 14.2 us -> 0.64 us
  matrix products: 12.1 us -> 0 us
  starting transfers between devices: 7.34 us -> 0 us
  other arithmetic: 4.66 us -> 0 us
    pallas_call x0 -> x1, Pallas kernels: none -> 28.7 us  [body(): pl.pallas_call(lambda *refs: kernel(share_count, *refs), out_shape=[jax.S...]
    psum x1 -> x0, waiting for transfers between devices: 17 us -> none  [expert_block(): totals = lax.psum(partial_sums, 'tp')]
    all_to_all x1 -> x0, blocking collectives: 15.7 us -> none  [body(): lax.all_to_all(outgoing, 'ep', split_axis=0, concat_axis=0, tiled=True)]
    dot_general x2 -> x0, matrix products: 12.1 us -> none  [the longest x1 7.86 us: expert_block(): jnp.einsum('smd,dh->smh', received, gate_block, preferred_element_type=jn...]
    all_to_all x1 -> x0, waiting for transfers between devices: 8.8 us -> none  [body(): lax.all_to_all(expert_block(received, gate_block, down_block), 'ep', spli...]
    all_to_all x1 -> x0, starting transfers between devices: 5.77 us -> none  [body(): lax.all_to_all(expert_block(received, gate_block, down_block), 'ep', spli...]
    psum x2 -> x0, blocking collectives: 5.06 us -> none  [rms_scale(): totals = lax.psum(jnp.sum(values * values, axis=1), 'tp')]
    squeeze x0 -> x2, local copies, waits for them, and re-layouts: none -> 2.67 us  [the longest x1 1.34 us: body(): routes[0]]
  transfers between devices with their start and end apart: 3 -> 0, of which waited for: 3 -> 0; matrix products, arithmetic and copies ran while one was open for 1% -> 0% of each run, Pallas kernels for 0% -> 0%
where the time goes in v1:
time: 35.1 us; the launch traced here: 34.8 us
  Pallas kernels  28.7 us (82%)
  local copies, waits for them, and re-layouts  5.41 us (15%)
  between operations  0.64 us (2%)
    pallas_call x1, Pallas kernels, body(): pl.pallas_call(lambda *refs: kernel(share_count, *refs), out_shape=[jax.S...  28.7 us
    unnamed x2, local copies, waits for them, and re-layouts  2.74 us
    squeeze x1, local copies, waits for them, and re-layouts, body(): routes[0]  1.34 us
    squeeze x1, local copies, waits for them, and re-layouts, body(): route_weights[0]  1.34 us

profile of v1, /device:TPU:0, one launch (start us, length us, event | category | flops | bytes accessed | tf_op | source)
XLA Modules:
  0.0 34.8 jit_solution(17240925020536935007)
XLA Ops:
  0.6 1.3 %copy.9.refs_1_ = s32[4,2]{1,0:T(4,128)} copy(s32[4,2]{0,1:T(2,128)} %bitcast.12) | data formatting | bytes 64 | tf_op jit(solution)/shard_map/squeeze | solution.py:344
  2.0 1.3 %copy.10.refs_2_ = f32[4,2]{1,0:T(4,128)} copy(f32[4,2]{0,1:T(2,128)} %bitcast.13) | data formatting | bytes 64 | tf_op jit(solution)/shard_map/squeeze | solution.py:344
  3.3 28.7 %routed_layer.1 = (bf16[4,3584]{1,0:T(4,128)(2,1)}, bf16[4,3584]{1,0:T(4,128)(2,1)}) custom-call(bf16[4,3584]{1,0:T(4,128)(2,1)} %bitcast.9, s32[4,2]{1,0:T(4,128)} %copy.9.refs_1_, f32[4,2]{1,0:T(4,128)} %copy.10.refs_2_, bf16[1,3584]{1,0:T(2,128)(2,1)} %refs_3_.1, bf16[1,3584]{1,0:T(2,128)(2,1)} %refs_4_.1, bf16[3584,2048]{1,0:T(8,128)(2,1)} %bitcast.7, ...), custom_call_target="tpu_custom_call" | custom-call | tf_op jit(solution)/shard_map/routed_layer/pallas_call | solution.py:304
  32.0 1.4 %copy.13 = bf16[1,4,3584]{2,1,0:T(4,128)(2,1)} copy(bf16[1,4,3584]{2,1,0:T(4,128)(2,1)} %bitcast.11) | data formatting | bytes 57344
  33.4 1.4 %copy.14 = bf16[1,4,3584]{2,1,0:T(4,128)(2,1)} copy(bf16[1,4,3584]{2,1,0:T(4,128)(2,1)} %bitcast.10) | data formatting | bytes 57344

commit v2 on v1

--- a/solution.py
+++ b/solution.py
@@ -55,7 +55,7 @@
     gain_far,
     lo_far,
     tot_own,
-    tot_tp,
+    weight_v,
     tot_far,
     tot_diag,
     gate_sem,
@@ -118,6 +118,14 @@
         pl.semaphore_signal(barrier, inc=1, device_id=target, device_id_type=MESH)
     gain_own[...] = out_gain_ref[...].astype(jnp.float32)
     rows_v[me] = x_ref[...]
+    named, weights = routes_ref[...], rw_ref[...]
+    corner = lax.broadcasted_iota(jnp.int32, (near, near), 0) == lax.broadcasted_iota(
+        jnp.int32, (near, near), 1
+    )
+    for expert in range(weight_v.shape[0]):
+        line = jnp.sum(jnp.where(named == expert, weights, 0.0), axis=0, keepdims=True)
+        column = jnp.sum(jnp.where(corner, line, 0.0), axis=1, keepdims=True)
+        weight_v[expert] = jnp.broadcast_to(column, (near, 128))
     pl.semaphore_wait(barrier, n + 2)
 
     def rows_copy(peer):
@@ -236,8 +244,6 @@
         looped(n - 1, send_ret)
         ret_v[me, :, low:high] = part_v[me, :, low:high]
 
-    named = routes_ref[...]
-    weights = rw_ref[...]
     squares = jnp.zeros((near, 1), jnp.float32)
     for part in range(2):
         low, high = bounds[part], bounds[part + 1]
@@ -249,9 +255,7 @@
         looped(n - 1, wait_ret)
 
         def add(at, total):
-            weight = jnp.sum(
-                jnp.where(named == at // share_count, weights, 0.0), axis=1, keepdims=True
-            )
+            weight = weight_v[at // share_count][:, :1]
             return total + weight * ret_v[at, :, low:high].astype(jnp.float32)
 
         mixture = looped(n, add, jnp.zeros((near, high - low), jnp.float32))
@@ -288,6 +292,17 @@
     looped(n - 1, drain)
 
 
+def deliver(lo_ref, handed_ref, lo_out, handed_out, sems):
+    copies = [
+        pltpu.make_async_copy(lo_ref, lo_out, sems.at[0]),
+        pltpu.make_async_copy(handed_ref, handed_out, sems.at[1]),
+    ]
+    for copy in copies:
+        copy.start()
+    for copy in copies:
+        copy.wait()
+
+
 def body(section_rows, routes, route_weights, in_gain, gate_up, down, out_gain):
     near, width = section_rows.shape[1:]
     hidden = down.shape[2]
@@ -303,7 +318,7 @@
     dma = pltpu.SemaphoreType.DMA
     layer_out, handed = pl.pallas_call(
         lambda *refs: kernel(share_count, *refs),
-        out_shape=[jax.ShapeDtypeStruct((near, width), bf16)] * 2,
+        out_shape=[pltpu.VMEM((near, width), bf16)] * 2,
         in_specs=[vmem] * 5 + [hbm] * 2,
         out_specs=[vmem] * 2,
         scratch_shapes=[
@@ -323,7 +338,7 @@
             pltpu.VMEM((1, width), f32),
             pltpu.VMEM((near, width), bf16),
             pltpu.VMEM((near, 128), f32),
-            pltpu.VMEM((near, 128), f32),
+            pltpu.VMEM((n // share_count, near, 128), f32),
             pltpu.VMEM((near, 128), f32),
             pltpu.VMEM((near, 128), f32),
             dma((pieces,)),
@@ -341,7 +356,15 @@
             collective_id=0, has_side_effects=True, vmem_limit_bytes=56 * 2**20
         ),
         name="routed_layer",
-    )(section_rows[0], routes[0], route_weights[0], in_gain, out_gain, gate_up[0, 0], down[0, 0])
+    )(section_rows[0], routes[0].T, route_weights[0].T, in_gain, out_gain, gate_up[0, 0], down[0, 0])
+    layer_out, handed = pl.pallas_call(
+        deliver,
+        out_shape=[jax.ShapeDtypeStruct((near, width), bf16)] * 2,
+        in_specs=[vmem] * 2,
+        out_specs=[hbm] * 2,
+        scratch_shapes=[dma((2,))],
+        name="deliver",
+    )(layer_out, handed)
     return (layer_out[None], handed[None])
 
 

time: 35.1 us -> 31.7 us (0.903)
  local copies, waits for them, and re-layouts: 5.41 us -> 1.2 us
  Pallas kernels: 28.7 us -> 29.6 us
    squeeze x2 -> x0, local copies, waits for them, and re-layouts: 2.67 us -> none  [the longest x1 1.34 us: body(): routes[0]]
    unnamed x2 -> x4, local copies, waits for them, and re-layouts: 2.74 us -> 1.2 us
    pallas_call x1 -> x2, Pallas kernels: 28.7 us -> 29.6 us  [the longest x1 28.2 us: body(): pl.pallas_call(lambda *refs: kernel(share_count, *refs), out_shape=[pltpu...]
where the time goes in v2:
time: 31.7 us; the launch traced here: 31.4 us
  Pallas kernels  29.6 us (93%)
  local copies, waits for them, and re-layouts  1.2 us (4%)
  between operations  0.65 us (2%)
    pallas_call x1, Pallas kernels, body(): pl.pallas_call(lambda *refs: kernel(share_count, *refs), out_shape=[pltpu...  28.2 us
    pallas_call x1, Pallas kernels, body(): pl.pallas_call(deliver, out_shape=[jax.ShapeDtypeStruct((near, width), bf...  1.4 us
    unnamed x4, local copies, waits for them, and re-layouts  1.2 us

profile of v2, /device:TPU:0, one launch (start us, length us, event | category | flops | bytes accessed | tf_op | source)
XLA Modules:
  0.0 31.4 jit_solution(11277681751655493557)
XLA Ops:
  0.6 28.2 %routed_layer.1 = (bf16[4,3584]{1,0:T(4,128)(2,1)S(1)}, bf16[4,3584]{1,0:T(4,128)(2,1)S(1)}) custom-call(bf16[4,3584]{1,0:T(4,128)(2,1)} %bitcast.13, s32[2,4]{1,0:T(2,128)} %bitcast.14, f32[2,4]{1,0:T(2,128)} %bitcast.15, bf16[1,3584]{1,0:T(2,128)(2,1)} %refs_3_.1, bf16[1,3584]{1,0:T(2,128)(2,1)} %refs_4_.1, bf16[3584,2048]{1,0:T(8,128)(2,1)} %bitcast.11, ...), custom_call_target="tpu_custom_call" | custom-call | tf_op jit(solution)/shard_map/routed_layer/pallas_call | solution.py:319
  28.8 0.0 copy-start
  28.8 0.6 %copy-done = bf16[4,3584]{1,0:T(4,128)(2,1)} copy-done((bf16[4,3584]{1,0:T(4,128)(2,1)}, bf16[4,3584]{1,0:T(4,128)(2,1)S(1)}, u32[]{:S(2)}) %copy-start) | copy-done | bytes 28696
  29.4 0.0 copy-start.1
  29.4 0.6 %copy-done.1 = bf16[4,3584]{1,0:T(4,128)(2,1)} copy-done((bf16[4,3584]{1,0:T(4,128)(2,1)}, bf16[4,3584]{1,0:T(4,128)(2,1)S(1)}, u32[]{:S(2)}) %copy-start.1) | copy-done | bytes 28696
  30.0 1.4 %deliver.1 = (bf16[4,3584]{1,0:T(4,128)(2,1)}, bf16[4,3584]{1,0:T(4,128)(2,1)}) custom-call(bf16[4,3584]{1,0:T(4,128)(2,1)} %copy-done, bf16[4,3584]{1,0:T(4,128)(2,1)} %copy-done.1), custom_call_target="tpu_custom_call" | custom-call | tf_op jit(solution)/shard_map/deliver/pallas_call | solution.py:360
Async XLA Ops:
  28.8 0.6 %copy-start = (bf16[4,3584]{1,0:T(4,128)(2,1)}, bf16[4,3584]{1,0:T(4,128)(2,1)S(1)}, u32[]{:S(2)}) copy-start(bf16[4,3584]{1,0:T(4,128)(2,1)S(1)} %get-tuple-element.6.lo_ref) | copy-start | bytes 86020
  29.4 0.6 %copy-start.1 = (bf16[4,3584]{1,0:T(4,128)(2,1)}, bf16[4,3584]{1,0:T(4,128)(2,1)S(1)}, u32[]{:S(2)}) copy-start(bf16[4,3584]{1,0:T(4,128)(2,1)S(1)} %get-tuple-element.7.handed_ref) | copy-start | bytes 86020

commit v3 on v2

--- a/solution.py
+++ b/solution.py
@@ -30,15 +30,20 @@
 
 def kernel(
     share_count,
+    x_hbm,
+    routes_hbm,
+    rw_hbm,
+    in_gain_hbm,
+    out_gain_hbm,
+    gate_hbm,
+    down_hbm,
+    lo_ref,
+    handed_ref,
     x_ref,
     routes_ref,
     rw_ref,
     in_gain_ref,
     out_gain_ref,
-    gate_hbm,
-    down_hbm,
-    lo_ref,
-    handed_ref,
     gate_v,
     down_v,
     rows_v,
@@ -49,7 +54,10 @@
     sums_far,
     hidden_v,
     y_v,
+    own_v,
     part_v,
+    half_v,
+    sum_v,
     ret_v,
     gain_own,
     gain_far,
@@ -58,10 +66,14 @@
     weight_v,
     tot_far,
     tot_diag,
+    in_sem,
     gate_sem,
     down_sem,
     rows_send,
     rows_recv,
+    fwd_send,
+    half_send,
+    half_recv,
     ret_send,
     ret_recv,
     sums_send,
@@ -70,21 +82,59 @@
     small_recv,
 ):
     n = rows_v.shape[0]
-    rows, width = y_v.shape
+    planes = n // 2
+    width = y_v.shape[1]
     near = x_ref.shape[0]
     hidden = down_v.shape[0]
-    span = gate_v.shape[1]
     pieces = sums_own.shape[0]
     cut = sums_own.shape[2]
     model = 2 * width
+    half = pieces // 2
     section = lax.axis_index("section")
     me = lax.axis_index("ep")
     core = lax.axis_index("tp")
+    plane, side = me // 2, me % 2
+    buddy = {"ep": me + 1 - 2 * side}
     twin = {"tp": 1 - core}
     across = {"section": 1 - section}
     diagonal = {"section": 1 - section, "tp": 1 - core}
 
-    half = pieces // 2
+    def others(step, order=None):
+        if planes > 8:
+
+            def one(at, carry):
+                step((plane + 1 + at) % planes)
+                return carry
+
+            lax.fori_loop(0, planes - 1, one, 0)
+            return
+        for offset in order or range(planes - 1, 0, -1):
+            target, bit = plane, 1
+            while bit < planes:
+                if offset & bit:
+                    target = target + bit * (1 - 2 * ((plane // bit) % 2))
+                bit *= 2
+            step(target)
+
+    x_copy = pltpu.make_async_copy(x_hbm, x_ref, in_sem.at[0])
+    in_copies = [
+        pltpu.make_async_copy(routes_hbm, routes_ref, in_sem.at[1]),
+        pltpu.make_async_copy(rw_hbm, rw_ref, in_sem.at[2]),
+        pltpu.make_async_copy(in_gain_hbm, in_gain_ref, in_sem.at[3]),
+        pltpu.make_async_copy(out_gain_hbm, out_gain_ref, in_sem.at[4]),
+    ]
+    x_copy.start()
+    for copy in in_copies:
+        copy.start()
+
+    barrier = pltpu.get_barrier_semaphore()
+
+    def greet(target):
+        pl.semaphore_signal(barrier, inc=1, device_id=target, device_id_type=MESH)
+
+    others(lambda to: greet({"ep": to * 2 + side}))
+    for target in (buddy, twin, across, diagonal):
+        greet(target)
 
     def columns(at):
         start = (at // 2) * cut + (at % 2) * hidden
@@ -104,20 +154,41 @@
     ]
     for copy in gate_copies + down_copies:
         copy.start()
-
-    barrier = pltpu.get_barrier_semaphore()
-
-    def greet(step, carry):
-        pl.semaphore_signal(
-            barrier, inc=1, device_id={"ep": (me + 1 + step) % n}, device_id_type=MESH
-        )
-        return carry
-
-    looped(n - 1, greet)
-    for target in (twin, across, diagonal):
-        pl.semaphore_signal(barrier, inc=1, device_id=target, device_id_type=MESH)
+    x_copy.wait()
+    pl.semaphore_wait(barrier, planes + 3)
+
+    def rows_copy(to):
+        return remote(
+            x_ref, rows_v.at[me], rows_send.at[to], rows_recv.at[me], {"ep": to * 2 + side}
+        )
+
+    def rows_arrival(of, side_of):
+        slot = of * 2 + side_of
+        return remote(x_ref, rows_v.at[slot], rows_send.at[of], rows_recv.at[slot], buddy)
+
+    def forward(of):
+        slot = of * 2 + side
+        return remote(
+            rows_v.at[slot], rows_v.at[slot], fwd_send.at[of], rows_recv.at[slot], buddy
+        )
+
+    own_copy = remote(x_ref, rows_v.at[me], fwd_send.at[plane], rows_recv.at[me], buddy)
+    others(lambda to: rows_copy(to).start())
+    own_copy.start()
+    rows_v[me] = x_ref[...]
+    for copy in in_copies:
+        copy.wait()
     gain_own[...] = out_gain_ref[...].astype(jnp.float32)
-    rows_v[me] = x_ref[...]
+    gain_copy = remote(gain_own, gain_far, small_send.at[0], small_recv.at[0], across)
+    gain_copy.start()
+
+    def pass_on(of):
+        rows_arrival(of, side).wait_recv()
+        forward(of).start()
+
+    early = [3, 1, 2] if planes == 4 else None
+    others(pass_on, early)
+
     named, weights = routes_ref[...], rw_ref[...]
     corner = lax.broadcasted_iota(jnp.int32, (near, near), 0) == lax.broadcasted_iota(
         jnp.int32, (near, near), 1
@@ -126,31 +197,9 @@
         line = jnp.sum(jnp.where(named == expert, weights, 0.0), axis=0, keepdims=True)
         column = jnp.sum(jnp.where(corner, line, 0.0), axis=1, keepdims=True)
         weight_v[expert] = jnp.broadcast_to(column, (near, 128))
-    pl.semaphore_wait(barrier, n + 2)
-
-    def rows_copy(peer):
-        return remote(
-            x_ref, rows_v.at[me], rows_send.at[peer], rows_recv.at[me], {"ep": peer}
-        )
-
-    def rows_arrival(peer):
-        return remote(
-            x_ref, rows_v.at[peer], rows_send.at[peer], rows_recv.at[peer], {"ep": peer}
-        )
-
-    def send_rows(step, carry):
-        rows_copy((me + 1 + step) % n).start()
-        return carry
-
-    looped(n - 1, send_rows)
-    gain_copy = remote(gain_own, gain_far, small_send.at[0], small_recv.at[0], across)
-    gain_copy.start()
-
-    def wait_rows(step, carry):
-        rows_arrival((me + 1 + step) % n).wait_recv()
-        return carry
-
-    looped(n - 1, wait_rows)
+
+    rows_arrival(plane, 1 - side).wait_recv()
+    others(lambda of: rows_arrival(of, 1 - side).wait_recv(), early)
 
     gain = in_gain_ref[...].astype(jnp.float32)
     group = 16 // near
@@ -198,27 +247,36 @@
     tiles = width // tile
     bounds = [0, (tiles + 1) // 2 * tile, width]
 
-    def ret_copy(peer, part):
+    def half_copy(to, part):
         where = slice(bounds[part], bounds[part + 1])
         return remote(
-            part_v.at[peer, :, where],
-            ret_v.at[me, :, where],
-            ret_send.at[part, peer],
-            ret_recv.at[part, me],
-            {"ep": peer},
-        )
-
-    def ret_arrival(peer, part):
+            part_v.at[to, :, where],
+            half_v.at[to, :, where],
+            half_send.at[part, to],
+            half_recv.at[part, to],
+            buddy,
+        )
+
+    def ret_copy(to, part):
         where = slice(bounds[part], bounds[part + 1])
         return remote(
-            part_v.at[peer, :, where],
-            ret_v.at[peer, :, where],
-            ret_send.at[part, peer],
-            ret_recv.at[part, peer],
-            {"ep": peer},
-        )
-
-    pair = 8 // near
+            sum_v.at[to, :, where],
+            ret_v.at[plane, :, where],
+            ret_send.at[part, to],
+            ret_recv.at[part, plane],
+            {"ep": to * 2 + side},
+        )
+
+    def ret_arrival(of, part):
+        where = slice(bounds[part], bounds[part + 1])
+        return remote(
+            sum_v.at[of, :, where],
+            ret_v.at[of, :, where],
+            ret_send.at[part, of],
+            ret_recv.at[part, of],
+            {"ep": of * 2 + side},
+        )
+
     for part in range(2):
         low, high = bounds[part], bounds[part + 1]
         for start in range(low, high, tile):
@@ -227,38 +285,46 @@
             )
 
         def split(at, carry):
-            where = pl.ds(at * 8 if isinstance(at, int) else pl.multiple_of(at * 8, 8), 8)
+            first = at * 2 * near
+            where = pl.ds(
+                first if isinstance(at, int) else pl.multiple_of(first, 2 * near), 2 * near
+            )
             block = y_v[where, low:high]
-            for i in range(pair):
-                part_v[at * pair + i, :, low:high] = block[i * near : (i + 1) * near].astype(
-                    jnp.bfloat16
-                )
+            even, odd = block[:near], block[near:]
+            own_v[at, :, low:high] = jnp.where(side == 0, even, odd)
+            part_v[at, :, low:high] = jnp.where(side == 0, odd, even).astype(jnp.bfloat16)
             return carry
 
-        looped(n // pair, split)
-
-        def send_ret(step, carry):
-            ret_copy((me + 1 + step) % n, part).start()
-            return carry
-
-        looped(n - 1, send_ret)
-        ret_v[me, :, low:high] = part_v[me, :, low:high]
+        looped(planes, split)
+        others(lambda to: half_copy(to, part).start())
+        half_copy(plane, part).start()
+
+    for part in range(2):
+        low, high = bounds[part], bounds[part + 1]
+
+        def joined(to):
+            half_copy(to, part).wait_recv()
+            return (own_v[to, :, low:high] + half_v[to, :, low:high].astype(jnp.float32)).astype(
+                jnp.bfloat16
+            )
+
+        def send_sum(to):
+            sum_v[to, :, low:high] = joined(to)
+            ret_copy(to, part).start()
+
+        others(send_sum)
+        ret_v[plane, :, low:high] = joined(plane)
 
     squares = jnp.zeros((near, 1), jnp.float32)
     for part in range(2):
         low, high = bounds[part], bounds[part + 1]
-
-        def wait_ret(step, carry):
-            ret_arrival((me + 1 + step) % n, part).wait_recv()
-            return carry
-
-        looped(n - 1, wait_ret)
+        others(lambda of: ret_arrival(of, part).wait_recv(), early)
 
         def add(at, total):
-            weight = weight_v[at // share_count][:, :1]
+            weight = weight_v[at // (share_count // 2)][:, :1]
             return total + weight * ret_v[at, :, low:high].astype(jnp.float32)
 
-        mixture = looped(n, add, jnp.zeros((near, high - low), jnp.float32))
+        mixture = looped(planes, add, jnp.zeros((near, high - low), jnp.float32))
         out = (x_ref[:, low:high].astype(jnp.float32) + mixture).astype(jnp.bfloat16)
         lo_ref[:, low:high] = out
         residual = out.astype(jnp.float32)
@@ -279,17 +345,19 @@
         jnp.bfloat16
     )
 
-    for copy in [gain_copy, sq_copy] + sums_copies + tail:
+    for copy in [gain_copy, sq_copy, own_copy] + sums_copies + tail:
         copy.wait_send()
 
-    def drain(step, carry):
-        peer = (me + 1 + step) % n
-        rows_copy(peer).wait_send()
+    def drain(to):
+        rows_copy(to).wait_send()
+        forward(to).wait_send()
         for part in range(2):
-            ret_copy(peer, part).wait_send()
-        return carry
-
-    looped(n - 1, drain)
+            half_copy(to, part).wait_send()
+            ret_copy(to, part).wait_send()
+
+    others(drain)
+    for part in range(2):
+        half_copy(plane, part).wait_send()
 
 
 def deliver(lo_ref, handed_ref, lo_out, handed_out, sems):
@@ -306,6 +374,7 @@
 def body(section_rows, routes, route_weights, in_gain, gate_up, down, out_gain):
     near, width = section_rows.shape[1:]
     hidden = down.shape[2]
+    topk = routes.shape[2]
     span = gate_up.shape[3]
     n = lax.axis_size("ep")
     share_count = min(16, n // 4)
@@ -319,9 +388,14 @@
     layer_out, handed = pl.pallas_call(
         lambda *refs: kernel(share_count, *refs),
         out_shape=[pltpu.VMEM((near, width), bf16)] * 2,
-        in_specs=[vmem] * 5 + [hbm] * 2,
+        in_specs=[hbm] * 7,
         out_specs=[vmem] * 2,
         scratch_shapes=[
+            pltpu.VMEM((near, width), bf16),
+            pltpu.VMEM((topk, near), jnp.int32),
+            pltpu.VMEM((topk, near), f32),
+            pltpu.VMEM((1, width), bf16),
+            pltpu.VMEM((1, width), bf16),
             pltpu.VMEM((width, span), bf16),
             pltpu.VMEM((hidden, width), bf16),
             pltpu.VMEM((n, near, width), bf16),
@@ -332,8 +406,11 @@
             pltpu.VMEM((pieces, rows, cut), f32),
             pltpu.VMEM((rows, hidden), bf16),
             pltpu.VMEM((rows, width), f32),
-            pltpu.VMEM((n, near, width), bf16),
-            pltpu.VMEM((n, near, width), bf16),
+            pltpu.VMEM((n // 2, near, width), f32),
+            pltpu.VMEM((n // 2, near, width), bf16),
+            pltpu.VMEM((n // 2, near, width), bf16),
+            pltpu.VMEM((n // 2, near, width), bf16),
+            pltpu.VMEM((n // 2, near, width), bf16),
             pltpu.VMEM((1, width), f32),
             pltpu.VMEM((1, width), f32),
             pltpu.VMEM((near, width), bf16),
@@ -341,19 +418,23 @@
             pltpu.VMEM((n // share_count, near, 128), f32),
             pltpu.VMEM((near, 128), f32),
             pltpu.VMEM((near, 128), f32),
+            dma((5,)),
             dma((pieces,)),
             dma((pieces // 2,)),
+            dma((n // 2,)),
             dma((n,)),
-            dma((n,)),
-            dma((2, n)),
-            dma((2, n)),
+            dma((n // 2,)),
+            dma((2, n // 2)),
+            dma((2, n // 2)),
+            dma((2, n // 2)),
+            dma((2, n // 2)),
             dma((pieces,)),
             dma((pieces,)),
             dma((5,)),
             dma((5,)),
         ],
         compiler_params=pltpu.CompilerParams(
-            collective_id=0, has_side_effects=True, vmem_limit_bytes=56 * 2**20
+            collective_id=0, has_side_effects=True, vmem_limit_bytes=60 * 2**20
         ),
         name="routed_layer",
     )(section_rows[0], routes[0].T, route_weights[0].T, in_gain, out_gain, gate_up[0, 0], down[0, 0])
@@ -363,6 +444,7 @@
         in_specs=[vmem] * 2,
         out_specs=[hbm] * 2,
         scratch_shapes=[dma((2,))],
+        compiler_params=pltpu.CompilerParams(vmem_limit_bytes=2 * 2**20),
         name="deliver",
     )(layer_out, handed)
     return (layer_out[None], handed[None])

time: 31.7 us -> 29.8 us (0.940)
  local copies, waits for them, and re-layouts: 1.2 us -> 0 us
  Pallas kernels: 29.6 us -> 29 us
    unnamed x4 -> x0, local copies, waits for them, and re-layouts: 1.2 us -> none
    pallas_call x1, Pallas kernels: 1.4 us -> 0.64 us  [body(): pl.pallas_call(deliver, out_shape=[jax.ShapeDtypeStruct((near, width), bf...]
where the time goes in v3:
time: 29.8 us; the launch traced here: 29.6 us
  Pallas kernels  29 us (97%)
  between operations  0.64 us (2%)
    pallas_call x1, Pallas kernels, body(): pl.pallas_call(lambda *refs: kernel(share_count, *refs), out_shape=[pltpu...  28.3 us
    pallas_call x1, Pallas kernels, body(): pl.pallas_call(deliver, out_shape=[jax.ShapeDtypeStruct((near, width), bf...  0.64 us

profile of v3, /device:TPU:0, one launch (start us, length us, event | category | flops | bytes accessed | tf_op | source)
XLA Modules:
  0.0 29.6 jit_solution(68372832877606975)
XLA Ops:
  0.6 28.3 %routed_layer.1 = (bf16[4,3584]{1,0:T(4,128)(2,1)S(1)}, bf16[4,3584]{1,0:T(4,128)(2,1)S(1)}) custom-call(bf16[4,3584]{1,0:T(4,128)(2,1)} %bitcast.13, s32[2,4]{1,0:T(2,128)} %bitcast.14, f32[2,4]{1,0:T(2,128)} %bitcast.15, bf16[1,3584]{1,0:T(2,128)(2,1)} %refs_3_.1, bf16[1,3584]{1,0:T(2,128)(2,1)} %refs_4_.1, bf16[3584,2048]{1,0:T(8,128)(2,1)} %bitcast.11, ...), custom_call_target="tpu_custom_call" | custom-call | tf_op jit(solution)/shard_map/routed_layer/pallas_call | solution.py:388
  29.0 0.6 %deliver.1 = (bf16[4,3584]{1,0:T(4,128)(2,1)}, bf16[4,3584]{1,0:T(4,128)(2,1)}) custom-call(bf16[4,3584]{1,0:T(4,128)(2,1)S(1)} %get-tuple-element.6.lo_ref, bf16[4,3584]{1,0:T(4,128)(2,1)S(1)} %get-tuple-element.7.handed_ref), custom_call_target="tpu_custom_call" | custom-call | tf_op jit(solution)/shard_map/deliver/pallas_call | solution.py:441

commit v4 on v3

--- a/solution.py
+++ b/solution.py
@@ -80,6 +80,8 @@
     sums_recv,
     small_send,
     small_recv,
+    lo_send,
+    lo_recv,
 ):
     n = rows_v.shape[0]
     planes = n // 2
@@ -198,13 +200,10 @@
         column = jnp.sum(jnp.where(corner, line, 0.0), axis=1, keepdims=True)
         weight_v[expert] = jnp.broadcast_to(column, (near, 128))
 
-    rows_arrival(plane, 1 - side).wait_recv()
-    others(lambda of: rows_arrival(of, 1 - side).wait_recv(), early)
-
     gain = in_gain_ref[...].astype(jnp.float32)
     group = 16 // near
 
-    def build(at, carry):
+    def build(at, carry=0):
         block = jnp.concatenate(
             [rows_v[at * group + i].astype(jnp.float32) for i in range(group)], axis=0
         )
@@ -214,7 +213,18 @@
         lhs_v[where, :] = (block * gain).astype(jnp.bfloat16)
         return carry
 
-    looped(n // group, build)
+    def wait_far(of):
+        rows_arrival(of, 1 - side).wait_recv()
+
+    wait_far(plane)
+    if n // group == 2 and planes == 4:
+        others(wait_far, [1])
+        build(plane // 2)
+        others(wait_far, [3, 2])
+        build(1 - plane // 2)
+    else:
+        others(wait_far)
+        looped(n // group, build)
     sq_copy = remote(sq_own, sq_far, small_send.at[1], small_recv.at[1], twin)
     sq_copy.start()
 
@@ -229,6 +239,20 @@
         )
         copy.start()
         sums_copies.append(copy)
+
+    tile = 512 if width % 512 == 0 else 128
+    third = max(1, width // tile * 3 // 7) * tile
+    bounds = [0, third, 2 * third, width]
+    parts = len(bounds) - 1
+
+    def down_step(at, start):
+        term = jnp.dot(
+            hidden_v[:, at * cut : (at + 1) * cut],
+            down_v[at * cut : (at + 1) * cut, start : start + tile],
+            preferred_element_type=jnp.float32,
+        )
+        where = slice(start, start + tile)
+        y_v[:, where] = term if at == 0 else y_v[:, where] + term
 
     sq_copy.wait_recv()
     scale = lax.rsqrt((sq_own[:, :1] + sq_far[:, :1]) / model + EPS)
@@ -240,12 +264,10 @@
         hidden_v[:, at * cut : (at + 1) * cut] = (a / (1.0 + jnp.exp(-a)) * b).astype(
             jnp.bfloat16
         )
-    for copy in down_copies:
-        copy.wait()
-
-    tile = 512 if width % 512 == 0 else 128
-    tiles = width // tile
-    bounds = [0, (tiles + 1) // 2 * tile, width]
+        down_copies[at].wait()
+        if at < half - 1:
+            for start in range(0, width, tile):
+                down_step(at, start)
 
     def half_copy(to, part):
         where = slice(bounds[part], bounds[part + 1])
@@ -277,12 +299,10 @@
             {"ep": of * 2 + side},
         )
 
-    for part in range(2):
+    def produce(part):
         low, high = bounds[part], bounds[part + 1]
         for start in range(low, high, tile):
-            y_v[:, start : start + tile] = jnp.dot(
-                hidden_v[...], down_v[:, start : start + tile], preferred_element_type=jnp.float32
-            )
+            down_step(half - 1, start)
 
         def split(at, carry):
             first = at * 2 * near
@@ -299,7 +319,7 @@
         others(lambda to: half_copy(to, part).start())
         half_copy(plane, part).start()
 
-    for part in range(2):
+    def combine(part):
         low, high = bounds[part], bounds[part + 1]
 
         def joined(to):
@@ -315,8 +335,20 @@
         others(send_sum)
         ret_v[plane, :, low:high] = joined(plane)
 
+    for part in range(parts):
+        produce(part)
+        if part > 0:
+            combine(part - 1)
+    combine(parts - 1)
+
+    def lo_copy(part):
+        where = slice(bounds[part], bounds[part + 1])
+        return remote(
+            lo_ref.at[:, where], lo_far.at[:, where], lo_send.at[part], lo_recv.at[part], across
+        )
+
     squares = jnp.zeros((near, 1), jnp.float32)
-    for part in range(2):
+    for part in range(parts):
         low, high = bounds[part], bounds[part + 1]
         others(lambda of: ret_arrival(of, part).wait_recv(), early)
 
@@ -327,19 +359,21 @@
         mixture = looped(planes, add, jnp.zeros((near, high - low), jnp.float32))
         out = (x_ref[:, low:high].astype(jnp.float32) + mixture).astype(jnp.bfloat16)
         lo_ref[:, low:high] = out
+        lo_copy(part).start()
         residual = out.astype(jnp.float32)
         squares = squares + jnp.sum(residual * residual, axis=1, keepdims=True)
     tot_own[...] = jnp.broadcast_to(squares, tot_own.shape)
     tail = [
-        remote(lo_ref, lo_far, small_send.at[2], small_recv.at[2], across),
-        remote(tot_own, tot_far, small_send.at[3], small_recv.at[3], across),
-        remote(tot_own, tot_diag, small_send.at[4], small_recv.at[4], diagonal),
+        remote(tot_own, tot_far, small_send.at[2], small_recv.at[2], across),
+        remote(tot_own, tot_diag, small_send.at[3], small_recv.at[3], diagonal),
     ]
     for copy in tail:
         copy.start()
     gain_copy.wait_recv()
     for copy in tail:
         copy.wait_recv()
+    for part in range(parts):
+        lo_copy(part).wait_recv()
     final = lax.rsqrt((tot_far[:, :1] + tot_diag[:, :1]) / model + EPS)
     handed_ref[...] = (lo_far[...].astype(jnp.float32) * final * gain_far[...]).astype(
         jnp.bfloat16
@@ -351,13 +385,14 @@
     def drain(to):
         rows_copy(to).wait_send()
         forward(to).wait_send()
-        for part in range(2):
+        for part in range(parts):
             half_copy(to, part).wait_send()
             ret_copy(to, part).wait_send()
 
     others(drain)
-    for part in range(2):
+    for part in range(parts):
         half_copy(plane, part).wait_send()
+        lo_copy(part).wait_send()
 
 
 def deliver(lo_ref, handed_ref, lo_out, handed_out, sems):
@@ -424,14 +459,16 @@
             dma((n // 2,)),
             dma((n,)),
             dma((n // 2,)),
-            dma((2, n // 2)),
-            dma((2, n // 2)),
-            dma((2, n // 2)),
-            dma((2, n // 2)),
+            dma((3, n // 2)),
+            dma((3, n // 2)),
+            dma((3, n // 2)),
+            dma((3, n // 2)),
             dma((pieces,)),
             dma((pieces,)),
-            dma((5,)),
-            dma((5,)),
+            dma((4,)),
+            dma((4,)),
+            dma((3,)),
+            dma((3,)),
         ],
         compiler_params=pltpu.CompilerParams(
             collective_id=0, has_side_effects=True, vmem_limit_bytes=60 * 2**20

time: 29.8 us -> 32.7 us (1.097)
  Pallas kernels: 29 us -> 31.9 us
    pallas_call x1, Pallas kernels: 28.3 us -> 31.3 us  [body(): pl.pallas_call(lambda *refs: kernel(share_count, *refs), out_shape=[pltpu...]
where the time goes in v4:
time: 32.7 us; the launch traced here: 32.6 us
  Pallas kernels  31.9 us (98%)
  between operations  0.64 us (2%)
    pallas_call x1, Pallas kernels, body(): pl.pallas_call(lambda *refs: kernel(share_count, *refs), out_shape=[pltpu...  31.3 us

profile of v4, /device:TPU:0, one launch (start us, length us, event | category | flops | bytes accessed | tf_op | source)
XLA Modules:
  0.0 32.6 jit_solution(3829979844742039996)
XLA Ops:
  0.6 31.3 %routed_layer.1 = (bf16[4,3584]{1,0:T(4,128)(2,1)S(1)}, bf16[4,3584]{1,0:T(4,128)(2,1)S(1)}) custom-call(bf16[4,3584]{1,0:T(4,128)(2,1)} %bitcast.13, s32[2,4]{1,0:T(2,128)} %bitcast.14, f32[2,4]{1,0:T(2,128)} %bitcast.15, bf16[1,3584]{1,0:T(2,128)(2,1)} %refs_3_.1, bf16[1,3584]{1,0:T(2,128)(2,1)} %refs_4_.1, bf16[3584,2048]{1,0:T(8,128)(2,1)} %bitcast.11, ...), custom_call_target="tpu_custom_call" | custom-call | tf_op jit(solution)/shard_map/routed_layer/pallas_call | solution.py:423
  31.9 0.6 %deliver.1 = (bf16[4,3584]{1,0:T(4,128)(2,1)}, bf16[4,3584]{1,0:T(4,128)(2,1)}) custom-call(bf16[4,3584]{1,0:T(4,128)(2,1)S(1)} %get-tuple-element.6.lo_ref, bf16[4,3584]{1,0:T(4,128)(2,1)S(1)} %get-tuple-element.7.handed_ref), custom_call_target="tpu_custom_call" | custom-call | tf_op jit(solution)/shard_map/deliver/pallas_call | solution.py:478

commit v5 on v3

--- a/solution.py
+++ b/solution.py
@@ -48,8 +48,6 @@
     down_v,
     rows_v,
     lhs_v,
-    sq_own,
-    sq_far,
     sums_own,
     sums_far,
     hidden_v,
@@ -86,8 +84,8 @@
     width = y_v.shape[1]
     near = x_ref.shape[0]
     hidden = down_v.shape[0]
-    pieces = sums_own.shape[0]
-    cut = sums_own.shape[2]
+    pieces = 2 * sums_own.shape[0]
+    cut = hidden // sums_own.shape[0]
     model = 2 * width
     half = pieces // 2
     section = lax.axis_index("section")
@@ -198,145 +196,163 @@
         column = jnp.sum(jnp.where(corner, line, 0.0), axis=1, keepdims=True)
         weight_v[expert] = jnp.broadcast_to(column, (near, 128))
 
-    rows_arrival(plane, 1 - side).wait_recv()
-    others(lambda of: rows_arrival(of, 1 - side).wait_recv(), early)
-
     gain = in_gain_ref[...].astype(jnp.float32)
     group = 16 // near
 
-    def build(at, carry):
+    def build(at, carry=0):
         block = jnp.concatenate(
             [rows_v[at * group + i].astype(jnp.float32) for i in range(group)], axis=0
         )
         where = pl.ds(at * 16 if isinstance(at, int) else pl.multiple_of(at * 16, 16), 16)
         squares = jnp.sum(block * block, axis=1, keepdims=True)
-        sq_own[where, :] = jnp.broadcast_to(squares, (16, 128))
+        for at_half in range(half):
+            sums_own[at_half, where, 2 * cut :] = jnp.broadcast_to(squares, (16, 128))
         lhs_v[where, :] = (block * gain).astype(jnp.bfloat16)
         return carry
 
-    looped(n // group, build)
-    sq_copy = remote(sq_own, sq_far, small_send.at[1], small_recv.at[1], twin)
-    sq_copy.start()
+    def wait_far(of):
+        rows_arrival(of, 1 - side).wait_recv()
+
+    wait_far(plane)
+    if n // group == 2 and planes == 4:
+        others(wait_far, [1])
+        build(plane // 2)
+        others(wait_far, [3, 2])
+        build(1 - plane // 2)
+    else:
+        others(wait_far)
+        looped(n // group, build)
 
     sums_copies = []
     for at in range(pieces):
         gate_copies[at].wait()
-        sums_own[at] = jnp.dot(
+        place = slice(at % 2 * cut, (at % 2 + 1) * cut)
+        sums_own[at // 2, :, place] = jnp.dot(
             lhs_v[...], gate_v[:, columns(at)], preferred_element_type=jnp.float32
         )
-        copy = remote(
-            sums_own.at[at], sums_far.at[at], sums_send.at[at], sums_recv.at[at], twin
-        )
-        copy.start()
-        sums_copies.append(copy)
-
-    sq_copy.wait_recv()
-    scale = lax.rsqrt((sq_own[:, :1] + sq_far[:, :1]) / model + EPS)
+        if at % 2 == 1:
+            to = at // 2
+            copy = remote(
+                sums_own.at[to], sums_far.at[to], sums_send.at[to], sums_recv.at[to], twin
+            )
+            copy.start()
+            sums_copies.append(copy)
+
     for at in range(half):
-        sums_copies[2 * at].wait_recv()
-        sums_copies[2 * at + 1].wait_recv()
-        a = (sums_own[2 * at] + sums_far[2 * at]) * scale
-        b = (sums_own[2 * at + 1] + sums_far[2 * at + 1]) * scale
+        sums_copies[at].wait_recv()
+        squares = sums_own[at, :, 2 * cut :][:, :1] + sums_far[at, :, 2 * cut :][:, :1]
+        scale = lax.rsqrt(squares / model + EPS)
+        a = (sums_own[at, :, :cut] + sums_far[at, :, :cut]) * scale
+        b = (sums_own[at, :, cut : 2 * cut] + sums_far[at, :, cut : 2 * cut]) * scale
         hidden_v[:, at * cut : (at + 1) * cut] = (a / (1.0 + jnp.exp(-a)) * b).astype(
             jnp.bfloat16
         )
     for copy in down_copies:
         copy.wait()
 
+    middle = planes // 2
+
+    def half_copy(to):
+        where = pl.ds(to * middle, middle)
+        return remote(
+            part_v.at[where], half_v.at[where], half_send.at[to], half_recv.at[to], buddy
+        )
+
+    def ret_copy(to):
+        return remote(
+            sum_v.at[to], ret_v.at[plane], ret_send.at[to], ret_recv.at[plane], {"ep": to * 2 + side}
+        )
+
+    def ret_arrival(of):
+        return remote(
+            sum_v.at[of], ret_v.at[of], ret_send.at[of], ret_recv.at[of], {"ep": of * 2 + side}
+        )
+
+    def keep(at, block, where):
+        even, odd = block[:near], block[near:]
+        own_v[at, :, where] = jnp.where(side == 0, even, odd)
+        part_v[at, :, where] = jnp.where(side == 0, odd, even).astype(jnp.bfloat16)
+
     tile = 512 if width % 512 == 0 else 128
-    tiles = width // tile
-    bounds = [0, (tiles + 1) // 2 * tile, width]
-
-    def half_copy(to, part):
-        where = slice(bounds[part], bounds[part + 1])
-        return remote(
-            part_v.at[to, :, where],
-            half_v.at[to, :, where],
-            half_send.at[part, to],
-            half_recv.at[part, to],
-            buddy,
-        )
-
-    def ret_copy(to, part):
-        where = slice(bounds[part], bounds[part + 1])
-        return remote(
-            sum_v.at[to, :, where],
-            ret_v.at[plane, :, where],
-            ret_send.at[part, to],
-            ret_recv.at[part, plane],
-            {"ep": to * 2 + side},
-        )
-
-    def ret_arrival(of, part):
-        where = slice(bounds[part], bounds[part + 1])
-        return remote(
-            sum_v.at[of, :, where],
-            ret_v.at[of, :, where],
-            ret_send.at[part, of],
-            ret_recv.at[part, of],
-            {"ep": of * 2 + side},
-        )
-
-    for part in range(2):
-        low, high = bounds[part], bounds[part + 1]
-        for start in range(low, high, tile):
-            y_v[:, start : start + tile] = jnp.dot(
-                hidden_v[...], down_v[:, start : start + tile], preferred_element_type=jnp.float32
-            )
+    for start in range(0, width, tile):
+        where = slice(start, start + tile)
+        term = jnp.dot(hidden_v[...], down_v[:, where], preferred_element_type=jnp.float32)
+        if planes <= 8:
+            for at in range(planes):
+                keep(at, term[at * 2 * near : (at + 1) * 2 * near], where)
+        else:
+            y_v[:, where] = term
+    if planes > 8:
 
         def split(at, carry):
-            first = at * 2 * near
-            where = pl.ds(
-                first if isinstance(at, int) else pl.multiple_of(first, 2 * near), 2 * near
-            )
-            block = y_v[where, low:high]
-            even, odd = block[:near], block[near:]
-            own_v[at, :, low:high] = jnp.where(side == 0, even, odd)
-            part_v[at, :, low:high] = jnp.where(side == 0, odd, even).astype(jnp.bfloat16)
+            first = pl.multiple_of(at * 2 * near, 2 * near)
+            keep(at, y_v[pl.ds(first, 2 * near), :], slice(0, width))
             return carry
 
-        looped(planes, split)
-        others(lambda to: half_copy(to, part).start())
-        half_copy(plane, part).start()
-
-    for part in range(2):
-        low, high = bounds[part], bounds[part + 1]
-
-        def joined(to):
-            half_copy(to, part).wait_recv()
-            return (own_v[to, :, low:high] + half_v[to, :, low:high].astype(jnp.float32)).astype(
-                jnp.bfloat16
-            )
-
-        def send_sum(to):
-            sum_v[to, :, low:high] = joined(to)
-            ret_copy(to, part).start()
-
+        lax.fori_loop(0, planes, split, 0)
+    here = plane // middle
+    half_copy(1 - here).start()
+    half_copy(here).start()
+
+    def joined(to):
+        return (own_v[to] + half_v[to].astype(jnp.float32)).astype(jnp.bfloat16)
+
+    def send_sum(to):
+        sum_v[to] = joined(to)
+        ret_copy(to).start()
+
+    half_copy(1 - here).wait_recv()
+    if planes == 4:
+        others(send_sum, [3, 2])
+        half_copy(here).wait_recv()
+        others(send_sum, [1])
+    else:
+        half_copy(here).wait_recv()
         others(send_sum)
-        ret_v[plane, :, low:high] = joined(plane)
-
-    squares = jnp.zeros((near, 1), jnp.float32)
-    for part in range(2):
-        low, high = bounds[part], bounds[part + 1]
-        others(lambda of: ret_arrival(of, part).wait_recv(), early)
-
-        def add(at, total):
-            weight = weight_v[at // (share_count // 2)][:, :1]
-            return total + weight * ret_v[at, :, low:high].astype(jnp.float32)
-
-        mixture = looped(planes, add, jnp.zeros((near, high - low), jnp.float32))
-        out = (x_ref[:, low:high].astype(jnp.float32) + mixture).astype(jnp.bfloat16)
-        lo_ref[:, low:high] = out
-        residual = out.astype(jnp.float32)
-        squares = squares + jnp.sum(residual * residual, axis=1, keepdims=True)
-    tot_own[...] = jnp.broadcast_to(squares, tot_own.shape)
+    ret_v[plane] = joined(plane)
+
+    def weighted(at):
+        return weight_v[at // (share_count // 2)][:, :1] * ret_v[at].astype(jnp.float32)
+
+    total = x_ref[...].astype(jnp.float32)
+    if planes <= 8:
+        terms = [total + weighted(plane)]
+
+        def arrive(of):
+            ret_arrival(of).wait_recv()
+            terms.append(terms[-1] + weighted(of))
+
+        others(arrive, early)
+        total = terms[-1]
+    else:
+        others(lambda of: ret_arrival(of).wait_recv())
+        total = looped(planes, lambda at, carry: carry + weighted(at), total)
+    out = total.astype(jnp.bfloat16)
+    lo_ref[...] = out
+    residual = out.astype(jnp.float32)
+    lo_copy = remote(lo_ref, lo_far, small_send.at[1], small_recv.at[1], across)
+    lo_copy.start()
+    tot_own[...] = jnp.broadcast_to(
+        jnp.sum(residual * residual, axis=1, keepdims=True), tot_own.shape
+    )
     tail = [
-        remote(lo_ref, lo_far, small_send.at[2], small_recv.at[2], across),
-        remote(tot_own, tot_far, small_send.at[3], small_recv.at[3], across),
-        remote(tot_own, tot_diag, small_send.at[4], small_recv.at[4], diagonal),
+        remote(tot_own, tot_diag, small_send.at[3], small_recv.at[3], diagonal),
+        remote(tot_own, tot_far, small_send.at[2], small_recv.at[2], across),
+        lo_copy,
     ]
-    for copy in tail:
+    for copy in tail[:2]:
         copy.start()
+
+    def drain(to):
+        rows_copy(to).wait_send()
+        forward(to).wait_send()
+        ret_copy(to).wait_send()
+
+    others(drain)
+    half_copy(0).wait_send()
+    half_copy(1).wait_send()
+    for copy in [gain_copy, own_copy] + sums_copies:
+        copy.wait_send()
     gain_copy.wait_recv()
     for copy in tail:
         copy.wait_recv()
@@ -344,20 +360,8 @@
     handed_ref[...] = (lo_far[...].astype(jnp.float32) * final * gain_far[...]).astype(
         jnp.bfloat16
     )
-
-    for copy in [gain_copy, sq_copy, own_copy] + sums_copies + tail:
+    for copy in tail:
         copy.wait_send()
-
-    def drain(to):
-        rows_copy(to).wait_send()
-        forward(to).wait_send()
-        for part in range(2):
-            half_copy(to, part).wait_send()
-            ret_copy(to, part).wait_send()
-
-    others(drain)
-    for part in range(2):
-        half_copy(plane, part).wait_send()
 
 
 def deliver(lo_ref, handed_ref, lo_out, handed_out, sems):
@@ -400,10 +404,8 @@
             pltpu.VMEM((hidden, width), bf16),
             pltpu.VMEM((n, near, width), bf16),
             pltpu.VMEM((rows, width), bf16),
-            pltpu.VMEM((rows, 128), f32),
-            pltpu.VMEM((rows, 128), f32),
-            pltpu.VMEM((pieces, rows, cut), f32),
-            pltpu.VMEM((pieces, rows, cut), f32),
+            pltpu.VMEM((pieces // 2, rows, 2 * cut + 128), f32),
+            pltpu.VMEM((pieces // 2, rows, 2 * cut + 128), f32),
             pltpu.VMEM((rows, hidden), bf16),
             pltpu.VMEM((rows, width), f32),
             pltpu.VMEM((n // 2, near, width), f32),
@@ -424,14 +426,14 @@
             dma((n // 2,)),
             dma((n,)),
             dma((n // 2,)),
-            dma((2, n // 2)),
-            dma((2, n // 2)),
-            dma((2, n // 2)),
-            dma((2, n // 2)),
-            dma((pieces,)),
-            dma((pieces,)),
-            dma((5,)),
-            dma((5,)),
+            dma((2,)),
+            dma((2,)),
+            dma((n // 2,)),
+            dma((n // 2,)),
+            dma((pieces // 2,)),
+            dma((pieces // 2,)),
+            dma((4,)),
+            dma((4,)),
         ],
         compiler_params=pltpu.CompilerParams(
             collective_id=0, has_side_effects=True, vmem_limit_bytes=60 * 2**20

time: 29.8 us -> 30.3 us (1.017)
  Pallas kernels: 29 us -> 29.5 us
    pallas_call x1, Pallas kernels: 28.3 us -> 28.9 us  [body(): pl.pallas_call(lambda *refs: kernel(share_count, *refs), out_shape=[pltpu...]
where the time goes in v5:
time: 30.3 us; the launch traced here: 30.2 us
  Pallas kernels  29.5 us (97%)
  between operations  0.64 us (2%)
    pallas_call x1, Pallas kernels, body(): pl.pallas_call(lambda *refs: kernel(share_count, *refs), out_shape=[pltpu...  28.9 us
    pallas_call x1, Pallas kernels, body(): pl.pallas_call(deliver, out_shape=[jax.ShapeDtypeStruct((near, width), bf...  0.64 us

profile of v5, /device:TPU:0, one launch (start us, length us, event | category | flops | bytes accessed | tf_op | source)
XLA Modules:
  0.0 30.2 jit_solution(7498554320663605562)
XLA Ops:
  0.6 28.9 %routed_layer.1 = (bf16[4,3584]{1,0:T(4,128)(2,1)S(1)}, bf16[4,3584]{1,0:T(4,128)(2,1)S(1)}) custom-call(bf16[4,3584]{1,0:T(4,128)(2,1)} %bitcast.13, s32[2,4]{1,0:T(2,128)} %bitcast.14, f32[2,4]{1,0:T(2,128)} %bitcast.15, bf16[1,3584]{1,0:T(2,128)(2,1)} %refs_3_.1, bf16[1,3584]{1,0:T(2,128)(2,1)} %refs_4_.1, bf16[3584,2048]{1,0:T(8,128)(2,1)} %bitcast.11, ...), custom_call_target="tpu_custom_call" | custom-call | tf_op jit(solution)/shard_map/routed_layer/pallas_call | solution.py:392
  29.5 0.6 %deliver.1 = (bf16[4,3584]{1,0:T(4,128)(2,1)}, bf16[4,3584]{1,0:T(4,128)(2,1)}) custom-call(bf16[4,3584]{1,0:T(4,128)(2,1)S(1)} %get-tuple-element.6.lo_ref, bf16[4,3584]{1,0:T(4,128)(2,1)S(1)} %get-tuple-element.7.handed_ref), custom_call_target="tpu_custom_call" | custom-call | tf_op jit(solution)/shard_map/deliver/pallas_call | solution.py:443

commit v6 on v5

--- a/solution.py
+++ b/solution.py
@@ -81,13 +81,11 @@
 ):
     n = rows_v.shape[0]
     planes = n // 2
+    rows = lhs_v.shape[0]
     width = y_v.shape[1]
     near = x_ref.shape[0]
     hidden = down_v.shape[0]
-    pieces = 2 * sums_own.shape[0]
-    cut = hidden // sums_own.shape[0]
     model = 2 * width
-    half = pieces // 2
     section = lax.axis_index("section")
     me = lax.axis_index("ep")
     core = lax.axis_index("tp")
@@ -134,22 +132,19 @@
     for target in (buddy, twin, across, diagonal):
         greet(target)
 
-    def columns(at):
-        start = (at // 2) * cut + (at % 2) * hidden
-        return slice(start, start + cut)
-
-    gate_copies = [
-        pltpu.make_async_copy(
-            gate_hbm.at[:, columns(at)], gate_v.at[:, columns(at)], gate_sem.at[at]
-        )
-        for at in range(pieces)
-    ]
-    down_copies = [
-        pltpu.make_async_copy(
-            down_hbm.at[at * cut : (at + 1) * cut], down_v.at[at * cut : (at + 1) * cut], down_sem.at[at]
-        )
-        for at in range(half)
-    ]
+    def fetches(source, target, sems):
+        step = source.shape[0] // sems.shape[0]
+        return [
+            pltpu.make_async_copy(
+                source.at[at * step : (at + 1) * step],
+                target.at[at * step : (at + 1) * step],
+                sems.at[at],
+            )
+            for at in range(sems.shape[0])
+        ]
+
+    gate_copies = fetches(gate_hbm, gate_v, gate_sem)
+    down_copies = fetches(down_hbm, down_v, down_sem)
     for copy in gate_copies + down_copies:
         copy.start()
     x_copy.wait()
@@ -205,8 +200,8 @@
         )
         where = pl.ds(at * 16 if isinstance(at, int) else pl.multiple_of(at * 16, 16), 16)
         squares = jnp.sum(block * block, axis=1, keepdims=True)
-        for at_half in range(half):
-            sums_own[at_half, where, 2 * cut :] = jnp.broadcast_to(squares, (16, 128))
+        for at_part in range(2):
+            sums_own[at_part, where, hidden:] = jnp.broadcast_to(squares, (16, 128))
         lhs_v[where, :] = (block * gain).astype(jnp.bfloat16)
         return carry
 
@@ -223,30 +218,31 @@
         others(wait_far)
         looped(n // group, build)
 
+    for copy in gate_copies:
+        copy.wait()
     sums_copies = []
-    for at in range(pieces):
-        gate_copies[at].wait()
-        place = slice(at % 2 * cut, (at % 2 + 1) * cut)
-        sums_own[at // 2, :, place] = jnp.dot(
-            lhs_v[...], gate_v[:, columns(at)], preferred_element_type=jnp.float32
-        )
-        if at % 2 == 1:
-            to = at // 2
-            copy = remote(
-                sums_own.at[to], sums_far.at[to], sums_send.at[to], sums_recv.at[to], twin
-            )
-            copy.start()
-            sums_copies.append(copy)
-
-    for at in range(half):
-        sums_copies[at].wait_recv()
-        squares = sums_own[at, :, 2 * cut :][:, :1] + sums_far[at, :, 2 * cut :][:, :1]
-        scale = lax.rsqrt(squares / model + EPS)
-        a = (sums_own[at, :, :cut] + sums_far[at, :, :cut]) * scale
-        b = (sums_own[at, :, cut : 2 * cut] + sums_far[at, :, cut : 2 * cut]) * scale
-        hidden_v[:, at * cut : (at + 1) * cut] = (a / (1.0 + jnp.exp(-a)) * b).astype(
-            jnp.bfloat16
-        )
+    for at in range(2):
+        sums_own[at, :, :hidden] = jnp.dot(
+            lhs_v[...],
+            gate_v[:, at * hidden : (at + 1) * hidden],
+            preferred_element_type=jnp.float32,
+        )
+        copy = remote(
+            sums_own.at[at], sums_far.at[at], sums_send.at[at], sums_recv.at[at], twin
+        )
+        copy.start()
+        sums_copies.append(copy)
+
+    sums_copies[0].wait_recv()
+    squares = sums_own[0, :, hidden:][:, :1] + sums_far[0, :, hidden:][:, :1]
+    scale = lax.rsqrt(squares / model + EPS)
+    sums_copies[1].wait_recv()
+    cut = min(256, hidden)
+    for start in range(0, hidden, cut):
+        where = slice(start, start + cut)
+        a = (sums_own[0, :, where] + sums_far[0, :, where]) * scale
+        b = (sums_own[1, :, where] + sums_far[1, :, where]) * scale
+        hidden_v[:, where] = (a / (1.0 + jnp.exp(-a)) * b).astype(jnp.bfloat16)
     for copy in down_copies:
         copy.wait()
 
@@ -273,9 +269,9 @@
         own_v[at, :, where] = jnp.where(side == 0, even, odd)
         part_v[at, :, where] = jnp.where(side == 0, odd, even).astype(jnp.bfloat16)
 
-    tile = 512 if width % 512 == 0 else 128
+    tile = 1024 if rows <= 64 else 512
     for start in range(0, width, tile):
-        where = slice(start, start + tile)
+        where = slice(start, min(start + tile, width))
         term = jnp.dot(hidden_v[...], down_v[:, where], preferred_element_type=jnp.float32)
         if planes <= 8:
             for at in range(planes):
@@ -383,8 +379,6 @@
     n = lax.axis_size("ep")
     share_count = min(16, n // 4)
     rows = n * near
-    cut = min(512, hidden)
-    pieces = span // cut
     vmem = pl.BlockSpec(memory_space=pltpu.VMEM)
     hbm = pl.BlockSpec(memory_space=pl.ANY)
     f32, bf16 = jnp.float32, jnp.bfloat16
@@ -404,8 +398,8 @@
             pltpu.VMEM((hidden, width), bf16),
             pltpu.VMEM((n, near, width), bf16),
             pltpu.VMEM((rows, width), bf16),
-            pltpu.VMEM((pieces // 2, rows, 2 * cut + 128), f32),
-            pltpu.VMEM((pieces // 2, rows, 2 * cut + 128), f32),
+            pltpu.VMEM((2, rows, hidden + 128), f32),
+            pltpu.VMEM((2, rows, hidden + 128), f32),
             pltpu.VMEM((rows, hidden), bf16),
             pltpu.VMEM((rows, width), f32),
             pltpu.VMEM((n // 2, near, width), f32),
@@ -421,8 +415,8 @@
             pltpu.VMEM((near, 128), f32),
             pltpu.VMEM((near, 128), f32),
             dma((5,)),
-            dma((pieces,)),
-            dma((pieces // 2,)),
+            dma((8,)),
+            dma((4,)),
             dma((n // 2,)),
             dma((n,)),
             dma((n // 2,)),
@@ -430,8 +424,8 @@
             dma((2,)),
             dma((n // 2,)),
             dma((n // 2,)),
-            dma((pieces // 2,)),
-            dma((pieces // 2,)),
+            dma((2,)),
+            dma((2,)),
             dma((4,)),
             dma((4,)),
         ],

time: 30.3 us -> 29.6 us (0.977)
  Pallas kernels: 29.5 us -> 28.8 us
    pallas_call x1, Pallas kernels: 28.9 us -> 28.2 us  [body(): pl.pallas_call(lambda *refs: kernel(share_count, *refs), out_shape=[pltpu...]
where the time goes in v6:
time: 29.6 us; the launch traced here: 29.5 us
  Pallas kernels  28.8 us (97%)
  between operations  0.64 us (2%)
    pallas_call x1, Pallas kernels, body(): pl.pallas_call(lambda *refs: kernel(share_count, *refs), out_shape=[pltpu...  28.2 us
    pallas_call x1, Pallas kernels, body(): pl.pallas_call(deliver, out_shape=[jax.ShapeDtypeStruct((near, width), bf...  0.64 us

profile of v6, /device:TPU:0, one launch (start us, length us, event | category | flops | bytes accessed | tf_op | source)
XLA Modules:
  0.0 29.5 jit_solution(2707091088617239637)
XLA Ops:
  0.6 28.2 %routed_layer.1 = (bf16[4,3584]{1,0:T(4,128)(2,1)S(1)}, bf16[4,3584]{1,0:T(4,128)(2,1)S(1)}) custom-call(bf16[4,3584]{1,0:T(4,128)(2,1)} %bitcast.13, s32[2,4]{1,0:T(2,128)} %bitcast.14, f32[2,4]{1,0:T(2,128)} %bitcast.15, bf16[1,3584]{1,0:T(2,128)(2,1)} %refs_3_.1, bf16[1,3584]{1,0:T(2,128)(2,1)} %refs_4_.1, bf16[3584,2048]{1,0:T(8,128)(2,1)} %bitcast.11, ...), custom_call_target="tpu_custom_call" | custom-call | tf_op jit(solution)/shard_map/routed_layer/pallas_call | solution.py:386
  28.8 0.6 %deliver.1 = (bf16[4,3584]{1,0:T(4,128)(2,1)}, bf16[4,3584]{1,0:T(4,128)(2,1)}) custom-call(bf16[4,3584]{1,0:T(4,128)(2,1)S(1)} %get-tuple-element.6.lo_ref, bf16[4,3584]{1,0:T(4,128)(2,1)S(1)} %get-tuple-element.7.handed_ref), custom_call_target="tpu_custom_call" | custom-call | tf_op jit(solution)/shard_map/deliver/pallas_call | solution.py:437

commit v7 on v6

--- a/solution.py
+++ b/solution.py
@@ -15,6 +15,20 @@
             carry = step(at, carry)
         return carry
     return lax.fori_loop(0, count, step, carry)
+
+
+def product(left, right, columns):
+    depth = right.shape[0]
+    step = depth // 2 if depth % 512 == 0 else depth
+    terms = [
+        jnp.dot(
+            left[:, at : at + step],
+            right[at : at + step, columns],
+            preferred_element_type=jnp.float32,
+        )
+        for at in range(0, depth, step)
+    ]
+    return sum(terms[1:], terms[0])
 
 
 def remote(src, dst, send, recv, target):
@@ -222,11 +236,7 @@
         copy.wait()
     sums_copies = []
     for at in range(2):
-        sums_own[at, :, :hidden] = jnp.dot(
-            lhs_v[...],
-            gate_v[:, at * hidden : (at + 1) * hidden],
-            preferred_element_type=jnp.float32,
-        )
+        sums_own[at, :, :hidden] = product(lhs_v, gate_v, slice(at * hidden, (at + 1) * hidden))
         copy = remote(
             sums_own.at[at], sums_far.at[at], sums_send.at[at], sums_recv.at[at], twin
         )
@@ -272,7 +282,7 @@
     tile = 1024 if rows <= 64 else 512
     for start in range(0, width, tile):
         where = slice(start, min(start + tile, width))
-        term = jnp.dot(hidden_v[...], down_v[:, where], preferred_element_type=jnp.float32)
+        term = product(hidden_v, down_v, where)
         if planes <= 8:
             for at in range(planes):
                 keep(at, term[at * 2 * near : (at + 1) * 2 * near], where)

time: 29.6 us -> 29.6 us (level)
  no operation moved by 1% of the time
where the time goes in v7:
time: 29.6 us; the launch traced here: 29.5 us
  Pallas kernels  28.8 us (97%)
  between operations  0.64 us (2%)
    pallas_call x1, Pallas kernels, body(): pl.pallas_call(lambda *refs: kernel(share_count, *refs), out_shape=[pltpu...  28.2 us
    pallas_call x1, Pallas kernels, body(): pl.pallas_call(deliver, out_shape=[jax.ShapeDtypeStruct((near, width), bf...  0.64 us

profile of v7, /device:TPU:0, one launch (start us, length us, event | category | flops | bytes accessed | tf_op | source)
XLA Modules:
  0.0 29.5 jit_solution(7297234159975828408)
XLA Ops:
  0.6 28.2 %routed_layer.1 = (bf16[4,3584]{1,0:T(4,128)(2,1)S(1)}, bf16[4,3584]{1,0:T(4,128)(2,1)S(1)}) custom-call(bf16[4,3584]{1,0:T(4,128)(2,1)} %bitcast.13, s32[2,4]{1,0:T(2,128)} %bitcast.14, f32[2,4]{1,0:T(2,128)} %bitcast.15, bf16[1,3584]{1,0:T(2,128)(2,1)} %refs_3_.1, bf16[1,3584]{1,0:T(2,128)(2,1)} %refs_4_.1, bf16[3584,2048]{1,0:T(8,128)(2,1)} %bitcast.11, ...), custom_call_target="tpu_custom_call" | custom-call | tf_op jit(solution)/shard_map/routed_layer/pallas_call | solution.py:396
  28.8 0.6 %deliver.1 = (bf16[4,3584]{1,0:T(4,128)(2,1)}, bf16[4,3584]{1,0:T(4,128)(2,1)}) custom-call(bf16[4,3584]{1,0:T(4,128)(2,1)S(1)} %get-tuple-element.6.lo_ref, bf16[4,3584]{1,0:T(4,128)(2,1)S(1)} %get-tuple-element.7.handed_ref), custom_call_target="tpu_custom_call" | custom-call | tf_op jit(solution)/shard_map/deliver/pallas_call | solution.py:447
